TPU v7x, 256 devices: a whole 4x4x8 slice. The times are simulated.
256 devices in a mesh: ctx: 4 (over x), tp: 8 (over y, z_hi), dp: 8 (over z_lo, core).
Axes of the slice: x: 4, y: 4, z: 8 (z_hi: 2, z_lo: 4; z = z_hi * 4 + z_lo), core: 2. Of those that a mesh axis runs over, the one named last changes fastest.
Arguments:
- residual: bfloat16 [32768, 4096], P(('dp', 'ctx', 'tp')), parts along dimension 0, may hold values from -6 to 6
- queries: bfloat16 [32768, 4096], P(('dp', 'ctx'), 'tp'), parts along dimension 0, may hold values from -5 to 5
- key_value: bfloat16 [2, 32768, 512], P(None, ('dp', 'ctx'), 'tp'), parts along dimension 1, may hold values from -5 to 5
- out_proj: bfloat16 [4096, 4096], P('tp', 'ctx'), may hold values from -0.5 to 0.5
- norm_gain: float32 [4096], replicated, may hold values from 0.1 to 1.9
- expert_ids: int32 [32768, 8], P(('dp', 'ctx', 'tp')), parts along dimension 0, may hold values from 0 to 127, all different within a row; in each aligned block of 128 rows (0 to 127, 128 to 255, ...) at most 24 rows name the same one
- gate_weights: float32 [32768, 8], P(('dp', 'ctx', 'tp')), parts along dimension 0, may hold values from 0.2 to 1
- expert_in: bfloat16 [4, 2, 4096, 1536], P('ctx', None, None, 'tp'), may hold values from -0.09375 to 0.09375
- expert_down: bfloat16 [4, 1536, 4096], P('ctx', 'tp'), may hold values from -0.15625 to 0.15625
Outputs:
- layer_out: bfloat16 [32768, 4096], P(('dp', 'ctx', 'tp')), parts along dimension 0
There are 8 independent parts, one for each index of `dp`. A program takes and returns all parts, laid end to end along the dimension named above; an argument that names none is the same for every part. Nothing has to cross between parts.
Inputs may be any that keep to these rules, and one draw needn't show every extreme that they name: `expert_ids`: each row names 8 different experts; in the rows of one device no expert is named more than 24 times.
All inputs are finite; a program needn't handle non-finite values.
Results may differ from a plain program's by a relative error of at most 0.017.
Values may be sent and summed in bfloat16 or wider, within the bound.
A program may use at most 64 MiB of HBM per device.

v0:
```python
import jax
import jax.numpy as jnp
from jax import lax
from jax.sharding import PartitionSpec as P

HD = 128
TOP = 8
CAP = 24


def partner_2(array, axis, distance):
    return lax.ppermute(array, axis, [(i, i ^ 1 << distance) for i in range(lax.axis_size(axis))])


def attend_block(run_state, query_block, key_block, value_block, query_pos, key_pos, score_scale):
    run_max, run_total, run_sum = run_state
    scores = (
        jnp.einsum("hqd,kd->hqk", query_block, key_block, preferred_element_type=jnp.float32)
        * score_scale
    )
    allowed = key_pos[None, :] <= query_pos[:, None]
    scores = jnp.where(allowed[None], scores, -1e30)
    new_max = jnp.maximum(run_max, jnp.max(scores, axis=2))
    factor = jnp.exp(run_max - new_max)
    weights = jnp.exp(scores - new_max[:, :, None])
    new_total = run_total * factor + jnp.sum(weights, axis=2)
    update = jnp.einsum(
        "hqk,kd->hqd", weights.astype(jnp.bfloat16), value_block, preferred_element_type=jnp.float32
    )
    return (new_max, new_total, run_sum * factor[:, :, None] + update)


def body(
    residual,
    queries,
    key_value,
    out_proj,
    norm_gain,
    expert_ids,
    gate_weights,
    expert_in,
    expert_down,
):
    ctx_count = lax.axis_size("ctx")
    tp_count = lax.axis_size("tp")
    shard_rows = queries.shape[0]
    local_heads = queries.shape[1] // HD
    model_width = residual.shape[1]
    tok_rows = residual.shape[0]
    partner = partner_2(key_value, "tp", 0)
    is_lower = lax.axis_index("tp") % 2 == 0
    head_pairs = jnp.where(
        is_lower,
        jnp.concatenate([key_value, partner], axis=2),
        jnp.concatenate([partner, key_value], axis=2),
    )
    block_rows = min(512, shard_rows)
    query_blocks = shard_rows // block_rows
    query_first = lax.axis_index("ctx") * shard_rows
    grouped = queries.reshape(query_blocks, block_rows, local_heads, HD).transpose(0, 2, 1, 3)
    score_scale = HD ** (-0.5)
    start_state = (
        jnp.full((query_blocks, local_heads, block_rows), -1e30, jnp.float32),
        jnp.zeros((query_blocks, local_heads, block_rows), jnp.float32),
        jnp.zeros((query_blocks, local_heads, block_rows, HD), jnp.float32),
    )
    key_piece = lax.all_gather(head_pairs, "ctx", axis=1, tiled=True)
    key_count = key_piece.shape[1] // block_rows
    key_blocks = key_piece[0].reshape(key_count, block_rows, HD)
    value_blocks = key_piece[1].reshape(key_count, block_rows, HD)

    def per_query(query_index, all_states):
        one_state = tuple((member[query_index] for member in all_states))
        query_block = grouped[query_index]
        query_start = query_first + query_index * block_rows
        query_pos = query_start + jnp.arange(block_rows)

        def per_key(key_index, inner_state):
            key_start = key_index * block_rows
            key_pos = key_start + jnp.arange(block_rows)

            def compute_block(given_state):
                return attend_block(
                    given_state,
                    query_block,
                    key_blocks[key_index],
                    value_blocks[key_index],
                    query_pos,
                    key_pos,
                    score_scale,
                )

            def keep_block(given_state):
                return given_state

            return lax.cond(key_start <= query_start, compute_block, keep_block, inner_state)

        one_state = lax.fori_loop(0, key_count, per_key, one_state)
        return tuple(
            (
                lax.dynamic_update_index_in_dim(member, value_now, query_index, 0)
                for member, value_now in zip(all_states, one_state)
            )
        )

    final_max, final_total, final_sum = lax.fori_loop(0, query_blocks, per_query, start_state)
    attended = (
        (final_sum / final_total[..., None])
        .transpose(0, 2, 1, 3)
        .reshape(shard_rows, local_heads * HD)
        .astype(jnp.bfloat16)
    )
    proj_full = lax.all_gather(out_proj, "ctx", axis=1, tiled=True)
    mixed_out = lax.psum_scatter(
        jnp.dot(attended, proj_full, preferred_element_type=jnp.float32).astype(jnp.bfloat16),
        "tp",
        scatter_dimension=0,
        tiled=True,
    ).astype(jnp.float32)
    stream = (residual.astype(jnp.float32) + mixed_out).astype(jnp.bfloat16)
    stream_wide = lax.optimization_barrier(stream).astype(jnp.float32)
    mean_square = jnp.mean(stream_wide * stream_wide, axis=1, keepdims=True)
    normed = (stream_wide * lax.rsqrt(mean_square + 1e-06) * norm_gain).astype(jnp.bfloat16)
    experts_here = jnp.arange(ctx_count, dtype=jnp.int32)
    chosen = (expert_ids[:, :, None] == experts_here).astype(jnp.int32)
    flat_choice = chosen.reshape(tok_rows * TOP, ctx_count)
    slot_rank = (jnp.cumsum(flat_choice, axis=0) - flat_choice).reshape(tok_rows, TOP, ctx_count)
    slot_ids = jnp.arange(CAP, dtype=jnp.int32)
    placed = chosen[:, :, :, None] * (slot_rank[:, :, :, None] == slot_ids).astype(jnp.int32)
    selector = jnp.sum(placed, axis=1).astype(jnp.bfloat16)
    weighted = jnp.einsum(
        "tk,tkec->tec", gate_weights, placed.astype(jnp.float32), precision=lax.Precision.HIGHEST
    )
    packed = jnp.einsum("tec,td->ecd", selector, normed, preferred_element_type=jnp.float32).astype(
        jnp.bfloat16
    )
    outgoing = jnp.repeat(packed, tp_count, axis=0)
    rows_in = lax.all_to_all(outgoing, ("ctx", "tp"), split_axis=0, concat_axis=0, tiled=True)
    flat_rows = rows_in.reshape(-1, model_width)
    both_parts = jnp.einsum(
        "rd,gdh->grh", flat_rows, expert_in[0], preferred_element_type=jnp.float32
    )
    hidden = (jax.nn.silu(both_parts[0]) * both_parts[1]).astype(jnp.bfloat16)
    down_out = jnp.dot(hidden, expert_down[0], preferred_element_type=jnp.float32)
    partial_out = down_out.reshape(rows_in.shape).astype(jnp.bfloat16)
    returned = lax.all_to_all(partial_out, ("ctx", "tp"), split_axis=0, concat_axis=0, tiled=True)
    expert_out = jnp.sum(
        returned.reshape(ctx_count, tp_count, CAP, model_width), axis=1, dtype=jnp.float32
    ).astype(jnp.bfloat16)
    added = jnp.einsum(
        "tec,ecd->td", weighted, expert_out.astype(jnp.float32), precision=lax.Precision.HIGHEST
    )
    return (stream_wide + added).astype(jnp.bfloat16)


def solution(mesh):
    in_specs = (
        P(("dp", "ctx", "tp"), None),
        P(("dp", "ctx"), "tp"),
        P(None, ("dp", "ctx"), "tp"),
        P("tp", "ctx"),
        P(),
        P(("dp", "ctx", "tp"), None),
        P(("dp", "ctx", "tp"), None),
        P("ctx", None, None, "tp"),
        P("ctx", "tp", None),
    )
    out_specs = P(("dp", "ctx", "tp"), None)
    return jax.shard_map(body, mesh=mesh, in_specs=in_specs, out_specs=out_specs, check_vma=False)
```

profile of v0, /device:TPU:34, one launch (start us, length us, event | category | flops | bytes accessed | tf_op | source)
XLA Modules:
  0.0 697.1 jit_solution(11294982153830927902)
XLA Ops:
  6.5 6.3 collective-permute-start
  12.8 12.2 %collective-permute-done = bf16[2,1024,64]{1,2,0:T(8,128)(2,1)S(1)} collective-permute-done((bf16[2,1024,64]{1,2,0:T(8,128)(2,1)}, bf16[2,1024,64]{1,2,0:T(8,128)(2,1)S(1)}, u32[]{:S(2)}, u32[]{:S(2)}) %collective-permute-start) | collective-permute-done | bytes 262176 | tf_op jit(solution)/shard_map/ppermute | solution.py:12
  30.0 31.1 %all-gather.3.cloned.1.call-done = bf16[2,4096,128]{1,2,0:T(8,128)(2,1)} async-done(((bf16[2,1024,128]{1,2,0:T(8,128)(2,1)}), bf16[2,4096,128]{1,2,0:T(8,128)(2,1)}) %all-gather.3.cloned.1.call-update) | async-done | bytes 2097168 | tf_op jit(solution)/shard_map/all_gather | solution.py:67
  61.1 3.1 fusion.40
  70.2 60.7 %while.57 = (s32[]{:T(128)}, f32[2,4,512]{2,1,0:T(4,128)S(1)}, f32[2,4,512]{2,1,0:T(4,128)S(1)}, f32[2,4,512,128]{3,2,1,0:T(8,128)}, s32[]{:T(128)}, /*index=5*/...) while((s32[]{:T(128)}, f32[2,4,512]{2,1,0:T(4,128)S(1)}, ...), condition=%wide.region_7.8_spmd, body=%wide.region_0.7_spmd.sunk | while | flops 549196800 | bytes 31407224 | solution.py:106
  74.6 20.3 %while.58 = (s32[]{:T(128)}, f32[4,512]{1,0:T(4,128)S(1)}, f32[4,512]{1,0:T(4,128)S(1)}, f32[4,512,128]{2,1,0:T(8,128)}, s32[]{:T(128)}, /*index=5*/bf16[8,512,1...) while((s32[]{:T(128)}, f32[4,512]{1,0:T(4,128)S(1)}, ...), condition=%wide.region_6.6_spmd.clone.clone, body=%wide.region_1.5_spmd.clone.clone.sunk | while | flops 549196800 | bytes 25049464 | solution.py:98
  74.6 6.8 conditional.4
  78.0 2.5 fusion.8
  81.4 6.7 conditional.4
  88.1 6.7 conditional.4
  91.4 2.4 fusion.8
  101.7 26.9 %while.58 = (s32[]{:T(128)}, f32[4,512]{1,0:T(4,128)S(1)}, f32[4,512]{1,0:T(4,128)S(1)}, f32[4,512,128]{2,1,0:T(8,128)}, s32[]{:T(128)}, /*index=5*/bf16[8,512,1...) while((s32[]{:T(128)}, f32[4,512]{1,0:T(4,128)S(1)}, ...), condition=%wide.region_6.6_spmd.clone.clone, body=%wide.region_1.5_spmd.clone.clone.sunk | while | flops 549196800 | bytes 25049464 | solution.py:98
  101.7 6.7 conditional.4
  108.4 6.7 conditional.4
  115.0 6.7 conditional.4
  121.7 6.7 conditional.4
  134.6 10.3 %convolution_convert_fusion = bf16[1024,4096]{1,0:T(8,128)(2,1)} fusion(bf16[512,4096]{1,0:T(8,128)(2,1)} %all-gather.5.cloned.1.call-done, bf16[128,8,4,128]{3,2,1,0:T(4,128)(2,1)} %bitcast.113), kind=kOutput, calls=%fused_computation.31 | convolution fusion | flops 4299161600 | bytes 13631488 | tf_op jit(solution)/shard_map/dot_general | solution.py:115
  148.5 235.7 %reduce-scatter.2.cloned.1.call-done = bf16[128,4096]{1,0:T(8,128)(2,1)} async-done(((bf16[1024,4096]{1,0:T(8,128)(2,1)}), bf16[128,4096]{1,0:T(8,128)(2,1)}) %reduce-scatter.2.cloned.1.call-update) | async-done | bytes 1048592 | tf_op jit(solution)/shard_map/reduce_scatter | solution.py:114
  388.1 148.5 %all_to_all.10 = bf16[32,24,4096]{2,1,0:T(8,128)(2,1)S(1)} all-to-all(bf16[32,24,4096]{2,1,0:T(8,128)(2,1)S(1)} %bitcast.106), channel_id=1, replica_groups=mesh['ctx'=4,'tp'=8,'dp'=8] {'ctx','tp'}, dimensions={0} | all-to-all | bytes 12582912 | tf_op jit(solution)/shard_map/all_to_all | solution.py:138
  536.6 2.7 fusion.41
  541.3 5.9 convolution_convert_fusion.1
  547.2 7.4 %all-to-all-start.1 = ((bf16[32,24,4096]{2,1,0:T(8,128)(2,1)}), bf16[32,24,4096]{2,1,0:T(8,128)(2,1)}, u32[]{:S(2)}, u32[]{:S(2)}) async-start(bf16[32,24,4096]{2,1,0:T(8,128)(2,1)} %convolution_convert_fusion.1), calls=%async_computation.2 | async-start | bytes 12582912 | tf_op jit(solution)/shard_map/all_to_all | solution.py:146
  554.7 129.8 %all-to-all-done.1 = bf16[32,24,4096]{2,1,0:T(8,128)(2,1)} async-done(((bf16[32,24,4096]{2,1,0:T(8,128)(2,1)}), bf16[32,24,4096]{2,1,0:T(8,128)(2,1)}, u32[]{:S(2)}, u32[]{:S(2)}) %all-to-all-start.1) | async-done | bytes 6291488 | tf_op jit(solution)/shard_map/all_to_all | solution.py:146
  684.5 4.0 bitcast_reduce_fusion
  (175 shorter events, 81.5 us)
Async XLA Ops:
  6.5 530.1 %copy-start = (bf16[1,2,4096,192]{2,3,1,0:T(8,128)(2,1)S(1)}, bf16[1,2,4096,192]{2,3,1,0:T(8,128)(2,1)}, u32[]{:S(2)}) copy-start(bf16[1,2,4096,192]{2,3,1,0:T(8,128)(2,1)} %param.22) | copy-start | bytes 9437188
  6.5 54.5 %all-gather.3.cloned.1.call-start = ((), (), s32[]{:S(2)}) async-start(), calls=%async_computation.3 | async-start | bytes 2621440 | tf_op jit(solution)/shard_map/all_gather | solution.py:67
  6.5 18.5 %collective-permute-start = (bf16[2,1024,64]{1,2,0:T(8,128)(2,1)}, bf16[2,1024,64]{1,2,0:T(8,128)(2,1)S(1)}, u32[]{:S(2)}, u32[]{:S(2)}) collective-permute-start(bf16[2,1024,64]{1,2,0:T(8,128)(2,1)} %param.17), channel_id=1, source_target_pairs={{0,8},{8,0},{16,24},{24,16},{32,40},{40,32},{48,56},{56,48},{1,9},... | collective-permute-start | bytes 786440 | tf_op jit(solution)/shard_map/ppermute | solution.py:12
  27.1 107.5 %all-gather.5.cloned.1.call-start = ((), (), s32[]{:S(2)}) async-start(), calls=%async_computation.4 | async-start | bytes 5242880 | tf_op jit(solution)/shard_map/all_gather | solution.py:113
  27.8 356.3 %reduce-scatter.2.cloned.1.call-start = ((), (), s32[]{:S(2)}) async-start(), calls=%async_computation.5 | async-start | bytes 9437184 | tf_op jit(solution)/shard_map/reduce_scatter | solution.py:114
  74.9 3.1 copy-start.1
  80.4 1.0 copy-start.2
  81.6 3.0 copy-start.1
  87.1 1.0 copy-start.2
  88.3 3.0 copy-start.1
  93.8 1.0 copy-start.2
  101.9 3.0 copy-start.1
  107.4 1.0 copy-start.2
  108.6 3.0 copy-start.1
  114.1 1.0 copy-start.2
  115.3 3.0 copy-start.1
  120.8 1.0 copy-start.2
  122.0 3.0 copy-start.1
  127.4 1.0 copy-start.2
  145.6 241.3 %copy-start.9 = (f32[4096]{0:T(1024)S(1)}, f32[4096]{0:T(1024)}, u32[]{:S(2)}) copy-start(f32[4096]{0:T(1024)} %param.19) | copy-start | bytes 49156
  547.2 7.4 %copy-start.6 = (s32[128,8,4]{0,2,1:T(4,128)S(1)}, s32[128,8,4]{0,2,1:T(4,128)}, u32[]{:S(2)}) copy-start(s32[128,8,4]{0,2,1:T(4,128)} %copy-done.5) | copy-start | bytes 49156
  547.2 7.4 %copy-start.8 = (f32[128,8]{0,1:T(8,128)S(1)}, f32[128,8]{0,1:T(8,128)}, u32[]{:S(2)}) copy-start(f32[128,8]{0,1:T(8,128)} %param.21) | copy-start | bytes 12292
  547.2 137.3 %all-to-all-start.1 = ((bf16[32,24,4096]{2,1,0:T(8,128)(2,1)}), bf16[32,24,4096]{2,1,0:T(8,128)(2,1)}, u32[]{:S(2)}, u32[]{:S(2)}) async-start(bf16[32,24,4096]{2,1,0:T(8,128)(2,1)} %convolution_convert_fusion.1), calls=%async_computation.2 | async-start | bytes 12582912 | tf_op jit(solution)/shard_map/all_to_all | solution.py:146
  684.5 4.0 copy-start.4
  (3 other events, 2.3 us)
Sparse Core Ops, SparseCore 0:
  27.2 33.8 all-gather.2
  62.9 51.1 all-gather.4
  145.0 239.0 reduce-scatter.1
where the time goes:
time: 709 us; the launch traced here: 697 us
  waiting for transfers between devices  409 us (58%)
  blocking collectives  149 us (21%)
  matrix products  52.9 us (7%)
  local copies, waits for them, and re-layouts  38 us (5%)
  other arithmetic  20.5 us (3%)
  starting transfers between devices  13.8 us (2%)
  between operations  13.3 us (2%)
    reduce_scatter x1, waiting for transfers between devices, body(): lax.psum_scatter(jnp.dot(attended, proj_full, preferred_element_type=jnp....  236 us
    all_to_all x1, blocking collectives, body(): lax.all_to_all(outgoing, ('ctx', 'tp'), split_axis=0, concat_axis=0, tile...  149 us
    all_to_all x1, waiting for transfers between devices, body(): lax.all_to_all(partial_out, ('ctx', 'tp'), split_axis=0, concat_axis=0, t...  130 us
    all_gather x1, waiting for transfers between devices, body(): key_piece = lax.all_gather(head_pairs, 'ctx', axis=1, tiled=True)  31.1 us
    dot_general x7, matrix products, attend_block(): jnp.einsum('hqk,kd->hqd', weights.astype(jnp.bfloat16), value_block, pref...  17 us
    dot_general x7, matrix products, attend_block(): jnp.einsum('hqd,kd->hqk', query_block, key_block, preferred_element_type=...  14.5 us
  transfers between devices with their start and end apart: 5, of which 4 were waited for; matrix products, arithmetic and copies ran while one was open for 10% of the time, Pallas kernels for 0%

commit v1 on v0

v1 whole, which is shorter than its diff:
```python
import jax
import jax.numpy as jnp
from jax import lax
from jax.experimental import pallas as pl
from jax.experimental.pallas import tpu as pltpu
from jax.sharding import PartitionSpec as P

HD = 128
CAP = 24
D = 4096
HALF = D // 2
NX = 4
NY = 4
ROWS = 128
EROWS = NX * CAP
MESH = pl.DeviceIdType.MESH
BF = jnp.bfloat16
F32 = jnp.float32
SCALE2 = HD ** (-0.5) * 1.4426950408889634
NT = (((1,), (1,)), ((), ()))


def kernel(
    q_ref, kv_ref, w_ref, res_ref, gain_ref, ids_ref, gw_ref, ein_ref, ed_ref,
    out_ref,
    kvbuf, vext, q2, qown, qother, acc, mrow, att, wbuf, sbuf, rsbuf, stream,
    packed, xd, disp, down, ret, xsend, eb, einbuf, edbuf,
    loc, s_kv, r_kvz, r_kvx, s_q, r_q, s_w, r_wz, r_wx, r_ws,
    s_rs, r_rs, s_e, r_e, s_x, r_x, s_y, r_y, s_ry, r_ry, s_rx, r_rx,
):
    c = lax.axis_index("ctx")
    t = lax.axis_index("tp")
    d = lax.axis_index("dp")
    y = t // 2
    h = t % 2
    k = d % 2
    hp = 1 - h
    kp = 1 - k

    pair = {"ctx": c, "tp": 2 * y + hp, "dp": d}
    sib = {"ctx": c, "tp": t, "dp": d + 1 - 2 * k}

    def xpeer(o):
        return {"ctx": lax.rem(c + o, NX), "tp": t, "dp": d}

    def ypeer(o):
        return {"ctx": c, "tp": 2 * lax.rem(y + o, NY) + h, "dp": d}

    def rcopy(src, dst, ss, rs, dev):
        return pltpu.make_async_remote_copy(
            src_ref=src, dst_ref=dst, send_sem=ss, recv_sem=rs, device_id=dev, device_id_type=MESH
        )

    barrier = pltpu.get_barrier_semaphore()
    peers = [pair, sib] + [xpeer(o) for o in (1, 2, 3)] + [ypeer(o) for o in (1, 2, 3)]
    for dev in peers:
        pl.semaphore_signal(barrier, inc=1, device_id=dev, device_id_type=MESH)
    pl.semaphore_wait(barrier, len(peers))

    kv_pair = rcopy(kv_ref, kvbuf.at[c, :, h], s_kv.at[0], r_kvz, pair)
    kv_pair.start()

    def kv_own(o):
        return rcopy(kv_ref, kvbuf.at[c, :, h], s_kv.at[o], r_kvx.at[o - 1, 0], xpeer(o))

    def kv_fwd(o):
        return rcopy(
            kvbuf.at[c, :, hp], kvbuf.at[c, :, hp], s_kv.at[3 + o], r_kvx.at[o - 1, 1], xpeer(o)
        )

    for o in (1, 2, 3):
        pl.when(c + o < NX)(lambda o=o: kv_own(o).start())
    kv_loc = pltpu.make_async_copy(kv_ref, kvbuf.at[c, :, h], loc.at[0])
    kv_loc.start()
    q_loc = pltpu.make_async_copy(q_ref.at[:, h], qown, loc.at[1])
    q_loc.start()
    w_loc = pltpu.make_async_copy(w_ref, wbuf.at[h, c], loc.at[2])
    w_loc.start()
    ein_loc = pltpu.make_async_copy(ein_ref, einbuf.at[:, h], loc.at[3])
    ein_loc.start()
    ed_loc = pltpu.make_async_copy(ed_ref, edbuf.at[h], loc.at[4])
    ed_loc.start()

    vext[:, :, HD:] = jnp.ones((NX, 1024, HD), BF)

    def spread_q(src, which):
        for b in range(4):
            block = src[b]
            for j in range(4):
                q2[which, j, b] = block[:, j * HD : (j + 1) * HD]

    q_loc.wait()
    spread_q(qown, h)

    q_pair = rcopy(q_ref.at[:, hp], qother, s_q, r_q, pair)
    kv_loc.wait()
    kv_pair.wait_recv()
    q_pair.start()
    for o in (1, 2, 3):
        pl.when(c + o < NX)(lambda o=o: kv_fwd(o).start())

    def put_v(src):
        vext[src, :, :HD] = kvbuf[src, 1].reshape(HD, 1024).astype(F32).T.astype(BF)

    put_v(c)
    w_pair = rcopy(w_ref.at[k], wbuf.at[h, c, k], s_w.at[0], r_wz, pair)

    def w_own(o):
        return rcopy(w_ref.at[k], wbuf.at[h, c, k], s_w.at[o], r_wx.at[o - 1, 0], xpeer(o))

    def w_fwd(o):
        return rcopy(
            wbuf.at[hp, c, k], wbuf.at[hp, c, k], s_w.at[3 + o], r_wx.at[o - 1, 1], xpeer(o)
        )

    w_sib = rcopy(wbuf.at[hp, c, k], wbuf.at[hp, c, k], s_w.at[7], r_ws.at[0], sib)

    def w_sib_own(o):
        cs = lax.rem(c + NX - o, NX)
        return rcopy(wbuf.at[h, cs, k], wbuf.at[h, cs, k], s_w.at[7 + o], r_ws.at[o], sib)

    def w_sib_fwd(o):
        cs = lax.rem(c + NX - o, NX)
        return rcopy(wbuf.at[hp, cs, k], wbuf.at[hp, cs, k], s_w.at[10 + o], r_ws.at[3 + o], sib)

    ein_pair = rcopy(ein_ref.at[k], einbuf.at[k, h], s_e.at[0], r_e.at[0], pair)
    ed_pair = rcopy(ed_ref.at[k], edbuf.at[h, k], s_e.at[1], r_e.at[1], pair)
    ein_sib = rcopy(einbuf.at[k, hp], einbuf.at[k, hp], s_e.at[2], r_e.at[2], sib)
    ed_sib = rcopy(edbuf.at[hp, k], edbuf.at[hp, k], s_e.at[3], r_e.at[3], sib)

    row_at = lax.broadcasted_iota(jnp.int32, (4, ROWS, 256), 1).reshape(4 * ROWS, 256) + h * ROWS
    col_at = lax.broadcasted_iota(jnp.int32, (4 * ROWS, 256), 1)
    allowed = col_at <= row_at

    def diagonal(which):
        keys = kvbuf[c, 0].reshape(HD, 1024)
        for b in range(4):
            kl = (b + 1) * 256
            qs = q2[which, :, b].reshape(4 * ROWS, HD)
            s = jnp.dot(qs, keys[:, :kl], preferred_element_type=F32)
            last = jnp.where(allowed, s[:, kl - 256 :], -1e30)
            s = last if b == 0 else jnp.concatenate([s[:, : kl - 256], last], axis=1)
            top = jnp.broadcast_to(jnp.max(s, axis=1, keepdims=True) * SCALE2, (4 * ROWS, HD))
            p = jnp.exp2(s * SCALE2 - jnp.concatenate([top] * (kl // HD), axis=1)).astype(BF)
            acc[which, :, b] = jnp.dot(
                p, vext[c, :kl], preferred_element_type=F32
            ).reshape(4, ROWS, 2 * HD)
            mrow[which, :, b] = top.reshape(4, ROWS, HD)

    def full_block(which, src):
        keys = kvbuf[src, 0].reshape(HD, 1024)
        for j in range(4):
            qs = q2[which, j].reshape(4 * ROWS, HD)
            s = jnp.dot(qs, keys, preferred_element_type=F32)
            old = mrow[which, j].reshape(4 * ROWS, HD)
            top = jnp.maximum(old, jnp.max(s, axis=1, keepdims=True) * SCALE2)
            factor = jnp.exp2(old - top)
            p = jnp.exp2(s * SCALE2 - jnp.concatenate([top] * 8, axis=1)).astype(BF)
            update = jnp.dot(p, vext[src], preferred_element_type=F32)
            acc[which, j] = (
                acc[which, j].reshape(4 * ROWS, 2 * HD) * jnp.concatenate([factor] * 2, axis=1)
                + update
            ).reshape(4, ROWS, 2 * HD)
            mrow[which, j] = top.reshape(4, ROWS, HD)

    def group(g, carry):
        which = lax.rem(h + g, 2)

        @pl.when(g == 1)
        def _():
            q_pair.wait_recv()
            spread_q(qother, hp)
            w_pair.start()
            ein_pair.start()
            ed_pair.start()

        diagonal(which)

        @pl.when(g == 0)
        def _():
            for o in (1, 3, 2):
                w_own(o).start()

        def earlier(o, carry):
            src = c - o

            @pl.when(g == 0)
            def _():
                rcopy(
                    kv_ref, kvbuf.at[src, :, h], s_kv.at[o], r_kvx.at[o - 1, 0], xpeer(o)
                ).wait_recv()
                rcopy(
                    kv_ref, kvbuf.at[src, :, hp], s_kv.at[o], r_kvx.at[o - 1, 1], xpeer(o)
                ).wait_recv()
                put_v(src)

            full_block(which, src)
            return carry

        lax.fori_loop(1, c + 1, earlier, 0)
        return carry

    lax.fori_loop(0, 2, group, 0)

    for w in range(2):
        for j in range(4):
            whole = acc[w, j].reshape(4 * ROWS, 2 * HD)
            head = (whole[:, :HD] / whole[:, HD:]).astype(BF)
            att[:, :, (4 * w + j) * HD : (4 * w + j + 1) * HD] = head.reshape(4, ROWS, HD)

    w_pair.wait_recv()
    w_sib.start()
    for o in (1, 3, 2):
        w_fwd(o).start()
    for o in (1, 3, 2):
        w_own(o).wait_recv()
        w_sib_own(o).start()
    w_loc.wait()
    w_sib.wait_recv()

    def rs_copy(i, o):
        return rcopy(
            sbuf.at[i, lax.rem(y + o, NY)], rsbuf.at[o - 1, i], s_rs.at[i, o - 1],
            r_rs.at[i, o - 1], ypeer(o),
        )

    order = (0, 1, 3, 2)
    for i, o in enumerate(order):
        cs = lax.rem(c + NX - o, NX)
        if o:
            w_fwd(o).wait_recv()
            w_sib_fwd(o).start()
            w_sib_own(o).wait_recv()
            w_sib_fwd(o).wait_recv()

        def tile(n, carry, cs=cs, i=i):
            at = pl.ds(pl.multiple_of(n * 256, 256), 256)
            rows = att[...].reshape(4 * ROWS, 1024)
            w0 = jnp.concatenate([wbuf[0, cs, 0, :, at], wbuf[0, cs, 1, :, at]], axis=0)
            w1 = jnp.concatenate([wbuf[1, cs, 0, :, at], wbuf[1, cs, 1, :, at]], axis=0)
            part = jnp.dot(rows[:, :512], w0, preferred_element_type=F32)
            part = part + jnp.dot(rows[:, 512:], w1, preferred_element_type=F32)
            sbuf[i, :, :, at] = part.astype(BF).reshape(4, ROWS, 256)
            return carry

        lax.fori_loop(0, 4, tile, 0)
        for o2 in (2, 1, 3):
            rs_copy(i, o2).start()

    slot_at = lax.broadcasted_iota(jnp.int32, (ROWS, ROWS), 0)
    lane_at = lax.broadcasted_iota(jnp.int32, (ROWS, ROWS), 1)
    group_at = sum((slot_at >= n * CAP).astype(jnp.int32) for n in (1, 2, 3, 4))
    expert_at = group_at + c
    expert_at = jnp.where(expert_at >= NX, expert_at - NX, expert_at)
    expert_at = jnp.where(group_at == 4, -1, expert_at)
    match = jnp.zeros((ROWS, ROWS), F32)
    gate = jnp.zeros((ROWS, ROWS), F32)
    for n in range(8):
        hit = ids_ref[n : n + 1, :] == expert_at
        match = match + jnp.where(hit, 1.0, 0.0)
        gate = gate + jnp.where(hit, gw_ref[n : n + 1, :], 0.0)
    before = jnp.where(slot_at < lane_at, 1.0, 0.0).astype(BF)
    rank = jnp.dot(match.astype(BF), before, preferred_element_type=F32)
    want = (slot_at - group_at * CAP).astype(F32)
    chosen = jnp.where(rank == want, match, 0.0)
    weighted = (chosen * gate).T
    chosen = chosen.astype(BF)

    square = jnp.zeros((ROWS, 1), F32)
    for i, o in enumerate(order):
        cs = lax.rem(c + NX - o, NX)
        at = pl.ds(pl.multiple_of(cs * 1024, 1024), 1024)
        for o2 in (1, 2, 3):
            rs_copy(i, o2).wait_recv()
        total = sbuf[i, y].astype(F32)
        for o2 in (1, 2, 3):
            total = total + rsbuf[o2 - 1, i].astype(F32)
        block = (res_ref[:, at].astype(F32) + total).astype(BF)
        stream[:, at] = block
        wide = block.astype(F32)
        square = square + jnp.sum(wide * wide, axis=1, keepdims=True)
    inv = lax.rsqrt(square * (1.0 / D) + 1e-6)

    for half in range(2):
        for n in range(4):
            lo = half * HALF + n * 512
            normed = (
                stream[:, lo : lo + 512].astype(F32) * inv * gain_ref[:, lo : lo + 512]
            ).astype(BF)
            rows = jnp.dot(chosen, normed, preferred_element_type=F32)
            for o in range(NX):
                if half == 0:
                    xsend[o, :CAP, n * 512 : (n + 1) * 512] = rows[o * CAP : (o + 1) * CAP]
                else:
                    xsend[o, CAP:, n * 512 : (n + 1) * 512] = rows[o * CAP : (o + 1) * CAP]
    packed[...] = xsend[...].astype(BF)

    def x_copy(o):
        return rcopy(packed.at[o], xd.at[o - 1], s_x.at[o - 1], r_x.at[o - 1], xpeer(o))

    for o in (2, 1, 3):
        x_copy(o).start()
    ein_pair.wait_recv()
    ein_sib.start()
    for o in (1, 3, 2):
        x_copy(o).wait_recv()
    pieces = [packed[0].astype(F32)] + [xd[o - 1].astype(F32) for o in (1, 2, 3)]
    for half in range(2):
        rows = jnp.concatenate([p[half * CAP : (half + 1) * CAP] for p in pieces], axis=0)
        disp[0, :, half * HALF : (half + 1) * HALF] = rows.astype(BF)

    def y_copy(o):
        return rcopy(disp.at[0], disp.at[o], s_y.at[o - 1], r_y.at[o - 1], ypeer(o))

    for o in (2, 1, 3):
        y_copy(o).start()
    ed_pair.wait_recv()
    ed_sib.start()
    ein_loc.wait()
    ed_loc.wait()
    ein_sib.wait_recv()
    ed_sib.wait_recv()
    for o in (1, 3, 2):
        y_copy(o).wait_recv()

    def project_in(n):
        total = jnp.zeros((4 * EROWS, 384), F32)
        for kk in range(4):
            at = slice(kk * 1024, (kk + 1) * 1024)
            total = total + lax.dot_general(
                disp[:, :, at].reshape(4 * EROWS, 1024),
                einbuf[n, :, :, at].reshape(384, 1024),
                NT,
                preferred_element_type=F32,
            )
        return total

    gate_part = project_in(0)
    hidden = (gate_part / (1.0 + jnp.exp(-gate_part)) * project_in(1)).astype(BF)

    def down_tile(n, carry):
        at = pl.ds(pl.multiple_of(n * 512, 512), 512)
        weights = edbuf[:, :, :, at].reshape(384, 512)
        part = jnp.dot(hidden, weights, preferred_element_type=F32)
        down[:, :, at] = part.astype(BF).reshape(4, EROWS, 512)
        return carry

    lax.fori_loop(0, D // 512, down_tile, 0)

    def ry_copy(o):
        return rcopy(
            down.at[o], ret.at[o - 1], s_ry.at[o - 1], r_ry.at[o - 1], ypeer(NY - o)
        )

    for o in (2, 1, 3):
        ry_copy(o).start()
    for o in (1, 3, 2):
        ry_copy(o).wait_recv()
    for half in range(2):
        at = slice(half * HALF, (half + 1) * HALF)
        total = down[0, :, at].astype(F32)
        for o in (1, 2, 3):
            total = total + ret[o - 1, :, at].astype(F32)
        for o in range(NX):
            xsend[o, half * CAP : (half + 1) * CAP, :] = total[o * CAP : (o + 1) * CAP]
    x_copy(1).wait_send()
    x_copy(2).wait_send()
    x_copy(3).wait_send()
    packed[...] = xsend[...].astype(BF)

    def rx_copy(o):
        return rcopy(packed.at[o], eb.at[o - 1], s_rx.at[o - 1], r_rx.at[o - 1], xpeer(NX - o))

    for o in (2, 1, 3):
        rx_copy(o).start()
    high = weighted.astype(BF)
    rest = weighted - high.astype(F32)
    mid = rest.astype(BF)
    low = (rest - mid.astype(F32)).astype(BF)
    for o in (1, 3, 2):
        rx_copy(o).wait_recv()
    pieces = [packed[0].astype(F32)] + [eb[o - 1].astype(F32) for o in (1, 2, 3)]
    for half in range(2):
        at = slice(half * HALF, (half + 1) * HALF)
        rows = jnp.concatenate(
            [p[half * CAP : (half + 1) * CAP] for p in pieces]
            + [jnp.zeros((ROWS - EROWS, HALF), F32)],
            axis=0,
        ).astype(BF)
        added = (
            jnp.dot(high, rows, preferred_element_type=F32)
            + jnp.dot(mid, rows, preferred_element_type=F32)
            + jnp.dot(low, rows, preferred_element_type=F32)
        )
        out_ref[:, at] = (stream[:, at].astype(F32) + added).astype(BF)

    kv_pair.wait_send()
    for o in (1, 2, 3):

        @pl.when(c + o < NX)
        def _(o=o):
            kv_own(o).wait_send()
            kv_fwd(o).wait_send()

    q_pair.wait_send()
    w_pair.wait_send()
    w_sib.wait_send()
    for o in (1, 2, 3):
        w_own(o).wait_send()
        w_fwd(o).wait_send()
        w_sib_own(o).wait_send()
        w_sib_fwd(o).wait_send()
        for i in range(4):
            rs_copy(i, o).wait_send()
        y_copy(o).wait_send()
        ry_copy(o).wait_send()
        rx_copy(o).wait_send()
    ein_pair.wait_send()
    ed_pair.wait_send()
    ein_sib.wait_send()
    ed_sib.wait_send()


def body(residual, queries, key_value, out_proj, norm_gain, expert_ids, gate_weights, expert_in, expert_down):
    sem = pltpu.SemaphoreType.DMA
    vmem = pl.BlockSpec(memory_space=pltpu.VMEM)
    hbm = pl.BlockSpec(memory_space=pl.ANY)
    scratch = [
        pltpu.VMEM((NX, 2, 2, 64, 1024), BF),
        pltpu.VMEM((NX, 1024, 2 * HD), BF),
        pltpu.VMEM((2, 4, 4, ROWS, HD), BF),
        pltpu.VMEM((4, ROWS, 512), BF),
        pltpu.VMEM((4, ROWS, 512), BF),
        pltpu.VMEM((2, 4, 4, ROWS, 2 * HD), F32),
        pltpu.VMEM((2, 4, 4, ROWS, HD), F32),
        pltpu.VMEM((4, ROWS, 1024), BF),
        pltpu.VMEM((2, NX, 2, 256, 1024), BF),
        pltpu.VMEM((4, NY, ROWS, 1024), BF),
        pltpu.VMEM((3, 4, ROWS, 1024), BF),
        pltpu.VMEM((ROWS, D), BF),
        pltpu.VMEM((NX, 2 * CAP, HALF), BF),
        pltpu.VMEM((3, 2 * CAP, HALF), BF),
        pltpu.VMEM((NY, EROWS, D), BF),
        pltpu.VMEM((NY, EROWS, D), BF),
        pltpu.VMEM((3, EROWS, D), BF),
        pltpu.VMEM((NX, 2 * CAP, HALF), F32),
        pltpu.VMEM((3, 2 * CAP, HALF), BF),
        pltpu.VMEM((2, 2, 192, D), BF),
        pltpu.VMEM((2, 2, 96, D), BF),
        sem((5,)),
        sem((7,)), sem, sem((3, 2)),
        sem, sem,
        sem((14,)), sem, sem((3, 2)), sem((7,)),
        sem((4, 3)), sem((4, 3)),
        sem((4,)), sem((4,)),
        sem((3,)), sem((3,)), sem((3,)), sem((3,)),
        sem((3,)), sem((3,)), sem((3,)), sem((3,)),
    ]
    return pl.pallas_call(
        kernel,
        out_shape=jax.ShapeDtypeStruct((ROWS, D), BF),
        in_specs=[hbm, hbm, hbm, vmem, vmem, vmem, vmem, hbm, hbm],
        out_specs=vmem,
        scratch_shapes=scratch,
        compiler_params=pltpu.CompilerParams(
            collective_id=0, has_side_effects=True, vmem_limit_bytes=62 * 1024 * 1024
        ),
        name="layer",
    )(
        queries.reshape(4, 2, ROWS, 512),
        jnp.swapaxes(key_value, 1, 2),
        out_proj.reshape(2, 256, 1024),
        residual,
        norm_gain.reshape(1, D),
        expert_ids.T,
        gate_weights.T,
        jnp.swapaxes(expert_in[0], 1, 2),
        expert_down[0].reshape(2, 96, D),
    )


def solution(mesh):
    in_specs = (
        P(("dp", "ctx", "tp"), None),
        P(("dp", "ctx"), "tp"),
        P(None, ("dp", "ctx"), "tp"),
        P("tp", "ctx"),
        P(),
        P(("dp", "ctx", "tp"), None),
        P(("dp", "ctx", "tp"), None),
        P("ctx", None, None, "tp"),
        P("ctx", "tp", None),
    )
    out_specs = P(("dp", "ctx", "tp"), None)
    return jax.shard_map(body, mesh=mesh, in_specs=in_specs, out_specs=out_specs, check_vma=False)
```

time: 709 us -> 288 us (0.41)
  the two profiles are of different devices: /device:TPU:34 before, /device:TPU:164 now
where the time goes in v1:
time: 288 us
  Pallas kernels  286 us (99%)
    pallas_call x1, Pallas kernels, body(): pl.pallas_call(kernel, out_shape=jax.ShapeDtypeStruct((ROWS, D), BF), in_...  286 us

profile of v1, /device:TPU:164, one launch (start us, length us, event | category | flops | bytes accessed | tf_op | source)
XLA Modules:
  0.0 288.3 jit_solution(457467001036361525)
XLA Ops:
  0.0 286.0 %layer.1 = bf16[128,4096]{1,0:T(8,128)(2,1)} custom-call(bf16[4,2,128,512]{3,2,1,0:T(8,128)(2,1)} %bitcast.12, bf16[2,64,1024]{2,1,0:T(8,128)(2,1)} %bitcast.14, bf16[2,256,1024]{2,1,0:T(8,128)(2,1)} %bitcast.13, bf16[128,4096]{1,0:T(8,128)(2,1)} %res_ref.1, f32[1,4096]{1,0:T(1,128)} %bitcast.15, s32[8,128]{1,0:T(8,128)} %bitcast.16, f32[8,128]{1,0:T(8,128)} %bitcast.17, ...), custom_call_target="tpu_custom_call" | custom-call | tf_op jit(solution)/shard_map/layer/pallas_call | solution.py:459
  286.0 2.3 copy.11

commit v2 on v1

--- a/solution.py
+++ b/solution.py
@@ -23,10 +23,11 @@
 def kernel(
     q_ref, kv_ref, w_ref, res_ref, gain_ref, ids_ref, gw_ref, ein_ref, ed_ref,
     out_ref,
-    kvbuf, vext, q2, qown, qother, acc, mrow, att, wbuf, sbuf, rsbuf, stream,
-    packed, xd, disp, down, ret, xsend, eb, einbuf, edbuf,
+    kvbuf, vext, q2, qown, qother, acc, mrow, att, wbuf, sbuf, oph, rsbuf, stream,
+    xsend, packed, xd, disp, down, rop, rnb, back, eb, einbuf, edbuf,
     loc, s_kv, r_kvz, r_kvx, s_q, r_q, s_w, r_wz, r_wx, r_ws,
-    s_rs, r_rs, s_e, r_e, s_x, r_x, s_y, r_y, s_ry, r_ry, s_rx, r_rx,
+    s_op, r_op, s_rs, r_rs, s_e, r_e, s_sib, r_sib, s_x, r_x, s_y, r_y, s_yp, r_yp,
+    s_ro, r_ro, s_rn, r_rn, s_rx, r_rx,
 ):
     c = lax.axis_index("ctx")
     t = lax.axis_index("tp")
@@ -37,8 +38,12 @@
     hp = 1 - h
     kp = 1 - k
 
+    zl = d // 2
+    edge = (zl == 0) | (zl == 3)
     pair = {"ctx": c, "tp": 2 * y + hp, "dp": d}
     sib = {"ctx": c, "tp": t, "dp": d + 1 - 2 * k}
+    across = {"ctx": c, "tp": 2 * y + hp, "dp": (3 - zl) * 2 + k}
+    inner = {"ctx": c, "tp": t, "dp": (zl + 1 - 2 * (zl % 2)) * 2 + k}
 
     def xpeer(o):
         return {"ctx": lax.rem(c + o, NX), "tp": t, "dp": d}
@@ -51,8 +56,14 @@
             src_ref=src, dst_ref=dst, send_sem=ss, recv_sem=rs, device_id=dev, device_id_type=MESH
         )
 
+    sent = []
+
+    def go(copy):
+        copy.start()
+        sent.append(copy)
+
     barrier = pltpu.get_barrier_semaphore()
-    peers = [pair, sib] + [xpeer(o) for o in (1, 2, 3)] + [ypeer(o) for o in (1, 2, 3)]
+    peers = [pair, sib, across, inner] + [xpeer(o) for o in (1, 2, 3)] + [ypeer(o) for o in (1, 3)]
     for dev in peers:
         pl.semaphore_signal(barrier, inc=1, device_id=dev, device_id_type=MESH)
     pl.semaphore_wait(barrier, len(peers))
@@ -81,6 +92,13 @@
     ed_loc = pltpu.make_async_copy(ed_ref, edbuf.at[h], loc.at[4])
     ed_loc.start()
 
+    w_across = rcopy(w_ref.at[k], wbuf.at[h, c, k], s_w.at[0], r_wz, across)
+    w_inner = rcopy(wbuf.at[hp, c, k], wbuf.at[hp, c, k], s_w.at[14], r_wz, inner)
+
+    @pl.when(edge)
+    def _():
+        w_across.start()
+
     vext[:, :, HD:] = jnp.ones((NX, 1024, HD), BF)
 
     def spread_q(src, which):
@@ -103,8 +121,6 @@
         vext[src, :, :HD] = kvbuf[src, 1].reshape(HD, 1024).astype(F32).T.astype(BF)
 
     put_v(c)
-    w_pair = rcopy(w_ref.at[k], wbuf.at[h, c, k], s_w.at[0], r_wz, pair)
-
     def w_own(o):
         return rcopy(w_ref.at[k], wbuf.at[h, c, k], s_w.at[o], r_wx.at[o - 1, 0], xpeer(o))
 
@@ -123,10 +139,29 @@
         cs = lax.rem(c + NX - o, NX)
         return rcopy(wbuf.at[hp, cs, k], wbuf.at[hp, cs, k], s_w.at[10 + o], r_ws.at[3 + o], sib)
 
-    ein_pair = rcopy(ein_ref.at[k], einbuf.at[k, h], s_e.at[0], r_e.at[0], pair)
-    ed_pair = rcopy(ed_ref.at[k], edbuf.at[h, k], s_e.at[1], r_e.at[1], pair)
-    ein_sib = rcopy(einbuf.at[k, hp], einbuf.at[k, hp], s_e.at[2], r_e.at[2], sib)
-    ed_sib = rcopy(edbuf.at[hp, k], edbuf.at[hp, k], s_e.at[3], r_e.at[3], sib)
+    def e_part(ref_in, ref_down, j, side):
+        if j < 4:
+            return ref_in.at[k, j] if side is None else ref_in.at[k, side, j]
+        return ref_down.at[k, j - 4] if side is None else ref_down.at[side, k, j - 4]
+
+    def e_across(j):
+        return rcopy(
+            e_part(ein_ref, ed_ref, j, None), e_part(einbuf, edbuf, j, h),
+            s_e.at[0, j], r_e.at[j], across,
+        )
+
+    def e_inner(j):
+        part = e_part(einbuf, edbuf, j, hp)
+        return rcopy(part, part, s_e.at[1, j], r_e.at[j], inner)
+
+    def e_pass(j):
+        @pl.when(edge)
+        def _():
+            e_across(j).wait_recv()
+            e_inner(j).start()
+
+    ein_sib = rcopy(einbuf.at[k, hp], einbuf.at[k, hp], s_sib.at[0], r_sib.at[0], sib)
+    ed_sib = rcopy(edbuf.at[hp, k], edbuf.at[hp, k], s_sib.at[1], r_sib.at[1], sib)
 
     row_at = lax.broadcasted_iota(jnp.int32, (4, ROWS, 256), 1).reshape(4 * ROWS, 256) + h * ROWS
     col_at = lax.broadcasted_iota(jnp.int32, (4 * ROWS, 256), 1)
@@ -169,10 +204,20 @@
         @pl.when(g == 1)
         def _():
             q_pair.wait_recv()
+            @pl.when(jnp.logical_not(edge))
+            def _():
+                w_across.wait_recv()
+
+            for o in (1, 3, 2):
+                w_fwd(o).start()
+            w_sib.start()
+
+            @pl.when(edge)
+            def _():
+                for j in range(6):
+                    e_across(j).start()
+
             spread_q(qother, hp)
-            w_pair.start()
-            ein_pair.start()
-            ed_pair.start()
 
         diagonal(which)
 
@@ -180,6 +225,11 @@
         def _():
             for o in (1, 3, 2):
                 w_own(o).start()
+
+            @pl.when(edge)
+            def _():
+                w_across.wait_recv()
+                w_inner.start()
 
         def earlier(o, carry):
             src = c - o
@@ -208,20 +258,23 @@
             head = (whole[:, :HD] / whole[:, HD:]).astype(BF)
             att[:, :, (4 * w + j) * HD : (4 * w + j + 1) * HD] = head.reshape(4, ROWS, HD)
 
-    w_pair.wait_recv()
-    w_sib.start()
-    for o in (1, 3, 2):
-        w_fwd(o).start()
+    e_pass(0)
     for o in (1, 3, 2):
         w_own(o).wait_recv()
         w_sib_own(o).start()
     w_loc.wait()
     w_sib.wait_recv()
 
-    def rs_copy(i, o):
-        return rcopy(
-            sbuf.at[i, lax.rem(y + o, NY)], rsbuf.at[o - 1, i], s_rs.at[i, o - 1],
-            r_rs.at[i, o - 1], ypeer(o),
+    def op_copy(i, side):
+        return rcopy(
+            sbuf.at[i, lax.rem(y + 2, NY), :, pl.ds(512 * side, 512)], oph.at[side, i],
+            s_op.at[side, i], r_op.at[side, i], ypeer(1 + 2 * side),
+        )
+
+    def nb_copy(i, side):
+        return rcopy(
+            sbuf.at[i, lax.rem(y + 1 + 2 * side, NY)], rsbuf.at[side, i],
+            s_rs.at[side, i], r_rs.at[side, i], ypeer(1 + 2 * side),
         )
 
     order = (0, 1, 3, 2)
@@ -244,8 +297,18 @@
             return carry
 
         lax.fori_loop(0, 4, tile, 0)
-        for o2 in (2, 1, 3):
-            rs_copy(i, o2).start()
+        for side in range(2):
+            go(op_copy(i, side))
+    for i in range(4):
+        for side in range(2):
+            op_copy(i, side).wait_recv()
+            to = lax.rem(y + 1 + 2 * side, NY)
+            lo = 512 * side
+            sbuf[i, to, :, lo : lo + 512] = (
+                sbuf[i, to, :, lo : lo + 512].astype(F32) + oph[side, i].astype(F32)
+            ).astype(BF)
+            go(nb_copy(i, side))
+    e_pass(1)
 
     slot_at = lax.broadcasted_iota(jnp.int32, (ROWS, ROWS), 0)
     lane_at = lax.broadcasted_iota(jnp.int32, (ROWS, ROWS), 1)
@@ -270,66 +333,89 @@
     for i, o in enumerate(order):
         cs = lax.rem(c + NX - o, NX)
         at = pl.ds(pl.multiple_of(cs * 1024, 1024), 1024)
-        for o2 in (1, 2, 3):
-            rs_copy(i, o2).wait_recv()
-        total = sbuf[i, y].astype(F32)
-        for o2 in (1, 2, 3):
-            total = total + rsbuf[o2 - 1, i].astype(F32)
+        for side in range(2):
+            nb_copy(i, side).wait_recv()
+        total = sbuf[i, y].astype(F32) + rsbuf[0, i].astype(F32) + rsbuf[1, i].astype(F32)
         block = (res_ref[:, at].astype(F32) + total).astype(BF)
         stream[:, at] = block
         wide = block.astype(F32)
         square = square + jnp.sum(wide * wide, axis=1, keepdims=True)
+        if i in (1, 2):
+            e_pass(1 + i)
     inv = lax.rsqrt(square * (1.0 / D) + 1e-6)
 
+    def x_copy(half, o):
+        return rcopy(
+            packed.at[o, half], xd.at[o - 1, half], s_x.at[half, o - 1], r_x.at[half, o - 1], xpeer(o)
+        )
+
+    def y_copy(half, side):
+        return rcopy(
+            disp.at[half, 0], disp.at[half, 1 + 2 * side], s_y.at[half, side], r_y.at[half, side],
+            ypeer(1 + 2 * side),
+        )
+
+    def y_pass(half):
+        return rcopy(
+            disp.at[half, 1 + 2 * half], disp.at[half, 2], s_yp.at[half], r_yp.at[half],
+            ypeer(1 + 2 * half),
+        )
+
+    def merge(pieces, quarter, extra):
+        lo = (quarter % 2) * CAP
+        return jnp.concatenate([p[lo : lo + CAP] for p in pieces] + extra, axis=0).astype(BF)
+
+    def split(rows, quarter):
+        lo = (quarter % 2) * CAP
+        for o in range(NX):
+            xsend[o, lo : lo + CAP] = rows[o * CAP : (o + 1) * CAP]
+
     for half in range(2):
-        for n in range(4):
-            lo = half * HALF + n * 512
-            normed = (
-                stream[:, lo : lo + 512].astype(F32) * inv * gain_ref[:, lo : lo + 512]
-            ).astype(BF)
-            rows = jnp.dot(chosen, normed, preferred_element_type=F32)
-            for o in range(NX):
-                if half == 0:
-                    xsend[o, :CAP, n * 512 : (n + 1) * 512] = rows[o * CAP : (o + 1) * CAP]
-                else:
-                    xsend[o, CAP:, n * 512 : (n + 1) * 512] = rows[o * CAP : (o + 1) * CAP]
-    packed[...] = xsend[...].astype(BF)
-
-    def x_copy(o):
-        return rcopy(packed.at[o], xd.at[o - 1], s_x.at[o - 1], r_x.at[o - 1], xpeer(o))
-
-    for o in (2, 1, 3):
-        x_copy(o).start()
-    ein_pair.wait_recv()
-    ein_sib.start()
-    for o in (1, 3, 2):
-        x_copy(o).wait_recv()
-    pieces = [packed[0].astype(F32)] + [xd[o - 1].astype(F32) for o in (1, 2, 3)]
+        for quarter in (2 * half, 2 * half + 1):
+            at = slice(quarter * 1024, (quarter + 1) * 1024)
+            normed = (stream[:, at].astype(F32) * inv * gain_ref[:, at]).astype(BF)
+            split(jnp.dot(chosen, normed, preferred_element_type=F32), quarter)
+        packed[:, half] = xsend[...].astype(BF)
+        for o in (2, 1, 3):
+            go(x_copy(half, o))
+    e_pass(4)
     for half in range(2):
-        rows = jnp.concatenate([p[half * CAP : (half + 1) * CAP] for p in pieces], axis=0)
-        disp[0, :, half * HALF : (half + 1) * HALF] = rows.astype(BF)
-
-    def y_copy(o):
-        return rcopy(disp.at[0], disp.at[o], s_y.at[o - 1], r_y.at[o - 1], ypeer(o))
-
-    for o in (2, 1, 3):
-        y_copy(o).start()
-    ed_pair.wait_recv()
-    ed_sib.start()
+        for o in (1, 3, 2):
+            x_copy(half, o).wait_recv()
+        pieces = [packed[0, half].astype(F32)] + [xd[o, half].astype(F32) for o in range(3)]
+        for n in range(2):
+            disp[half, 0, :, n * 1024 : (n + 1) * 1024] = merge(pieces, n, [])
+        for side in range(2):
+            go(y_copy(half, side))
+    e_pass(5)
+
+    @pl.when(jnp.logical_not(edge))
+    def _():
+        for j in range(6):
+            e_inner(j).wait_recv()
+
+    go(ein_sib)
+    go(ed_sib)
+    y_copy(0, 0).wait_recv()
+    go(y_pass(0))
+    y_copy(1, 1).wait_recv()
+    go(y_pass(1))
     ein_loc.wait()
     ed_loc.wait()
     ein_sib.wait_recv()
     ed_sib.wait_recv()
-    for o in (1, 3, 2):
-        y_copy(o).wait_recv()
+    y_copy(0, 1).wait_recv()
+    y_copy(1, 0).wait_recv()
+    y_pass(0).wait_recv()
+    y_pass(1).wait_recv()
 
     def project_in(n):
         total = jnp.zeros((4 * EROWS, 384), F32)
         for kk in range(4):
-            at = slice(kk * 1024, (kk + 1) * 1024)
+            lo = (kk % 2) * 1024
             total = total + lax.dot_general(
-                disp[:, :, at].reshape(4 * EROWS, 1024),
-                einbuf[n, :, :, at].reshape(384, 1024),
+                disp[kk // 2, :, :, lo : lo + 1024].reshape(4 * EROWS, 1024),
+                einbuf[n, :, :, :, kk * 1024 : (kk + 1) * 1024].reshape(384, 1024),
                 NT,
                 preferred_element_type=F32,
             )
@@ -338,61 +424,75 @@
     gate_part = project_in(0)
     hidden = (gate_part / (1.0 + jnp.exp(-gate_part)) * project_in(1)).astype(BF)
 
-    def down_tile(n, carry):
-        at = pl.ds(pl.multiple_of(n * 512, 512), 512)
-        weights = edbuf[:, :, :, at].reshape(384, 512)
-        part = jnp.dot(hidden, weights, preferred_element_type=F32)
-        down[:, :, at] = part.astype(BF).reshape(4, EROWS, 512)
-        return carry
-
-    lax.fori_loop(0, D // 512, down_tile, 0)
-
-    def ry_copy(o):
-        return rcopy(
-            down.at[o], ret.at[o - 1], s_ry.at[o - 1], r_ry.at[o - 1], ypeer(NY - o)
-        )
-
-    for o in (2, 1, 3):
-        ry_copy(o).start()
-    for o in (1, 3, 2):
-        ry_copy(o).wait_recv()
+    def ro_copy(half):
+        return rcopy(
+            down.at[half, 2], rop.at[half], s_ro.at[half], r_ro.at[half], ypeer(1 + 2 * half)
+        )
+
+    def rn_copy(half, side):
+        return rcopy(
+            down.at[half, 3 - 2 * side], rnb.at[half, side], s_rn.at[half, side],
+            r_rn.at[half, side], ypeer(1 + 2 * side),
+        )
+
     for half in range(2):
-        at = slice(half * HALF, (half + 1) * HALF)
-        total = down[0, :, at].astype(F32)
-        for o in (1, 2, 3):
-            total = total + ret[o - 1, :, at].astype(F32)
-        for o in range(NX):
-            xsend[o, half * CAP : (half + 1) * CAP, :] = total[o * CAP : (o + 1) * CAP]
-    x_copy(1).wait_send()
-    x_copy(2).wait_send()
-    x_copy(3).wait_send()
-    packed[...] = xsend[...].astype(BF)
-
-    def rx_copy(o):
-        return rcopy(packed.at[o], eb.at[o - 1], s_rx.at[o - 1], r_rx.at[o - 1], xpeer(NX - o))
-
-    for o in (2, 1, 3):
-        rx_copy(o).start()
+
+        def down_tile(n, carry, half=half):
+            lo = pl.multiple_of(n * 512, 512)
+            weights = edbuf[:, :, :, :, pl.ds(half * HALF + lo, 512)].reshape(384, 512)
+            part = jnp.dot(hidden, weights, preferred_element_type=F32)
+            down[half, :, :, pl.ds(lo, 512)] = part.astype(BF).reshape(4, EROWS, 512)
+            return carry
+
+        lax.fori_loop(0, HALF // 512, down_tile, 0)
+        if half == 0:
+            go(ro_copy(0))
+            go(rn_copy(0, 1))
+        else:
+            go(ro_copy(1))
+    for half in range(2):
+        ro_copy(half).wait_recv()
+        slot = 3 - 2 * half
+        down[half, slot] = (down[half, slot].astype(F32) + rop[half].astype(F32)).astype(BF)
+        go(rn_copy(half, half))
+        if half == 0:
+            go(rn_copy(1, 0))
+
+    def rx_copy(half, o):
+        return rcopy(
+            back.at[o, half], eb.at[o - 1, half], s_rx.at[half, o - 1], r_rx.at[half, o - 1],
+            xpeer(NX - o),
+        )
+
+    for half in range(2):
+        for side in range(2):
+            rn_copy(half, side).wait_recv()
+        for n in range(2):
+            at = slice(n * 1024, (n + 1) * 1024)
+            total = down[half, 0, :, at].astype(F32)
+            for side in range(2):
+                total = total + rnb[half, side, :, at].astype(F32)
+            split(total, n)
+        back[:, half] = xsend[...].astype(BF)
+        for o in (2, 1, 3):
+            go(rx_copy(half, o))
     high = weighted.astype(BF)
     rest = weighted - high.astype(F32)
     mid = rest.astype(BF)
     low = (rest - mid.astype(F32)).astype(BF)
-    for o in (1, 3, 2):
-        rx_copy(o).wait_recv()
-    pieces = [packed[0].astype(F32)] + [eb[o - 1].astype(F32) for o in (1, 2, 3)]
     for half in range(2):
-        at = slice(half * HALF, (half + 1) * HALF)
-        rows = jnp.concatenate(
-            [p[half * CAP : (half + 1) * CAP] for p in pieces]
-            + [jnp.zeros((ROWS - EROWS, HALF), F32)],
-            axis=0,
-        ).astype(BF)
-        added = (
-            jnp.dot(high, rows, preferred_element_type=F32)
-            + jnp.dot(mid, rows, preferred_element_type=F32)
-            + jnp.dot(low, rows, preferred_element_type=F32)
-        )
-        out_ref[:, at] = (stream[:, at].astype(F32) + added).astype(BF)
+        for o in (1, 3, 2):
+            rx_copy(half, o).wait_recv()
+        pieces = [back[0, half].astype(F32)] + [eb[o, half].astype(F32) for o in range(3)]
+        for n in range(2):
+            at = slice(half * HALF + n * 1024, half * HALF + (n + 1) * 1024)
+            rows = merge(pieces, n, [jnp.zeros((ROWS - EROWS, 1024), F32)])
+            added = (
+                jnp.dot(high, rows, preferred_element_type=F32)
+                + jnp.dot(mid, rows, preferred_element_type=F32)
+                + jnp.dot(low, rows, preferred_element_type=F32)
+            )
+            out_ref[:, at] = (stream[:, at].astype(F32) + added).astype(BF)
 
     kv_pair.wait_send()
     for o in (1, 2, 3):
@@ -403,22 +503,23 @@
             kv_fwd(o).wait_send()
 
     q_pair.wait_send()
-    w_pair.wait_send()
     w_sib.wait_send()
     for o in (1, 2, 3):
         w_own(o).wait_send()
         w_fwd(o).wait_send()
         w_sib_own(o).wait_send()
         w_sib_fwd(o).wait_send()
-        for i in range(4):
-            rs_copy(i, o).wait_send()
-        y_copy(o).wait_send()
-        ry_copy(o).wait_send()
-        rx_copy(o).wait_send()
-    ein_pair.wait_send()
-    ed_pair.wait_send()
-    ein_sib.wait_send()
-    ed_sib.wait_send()
+
+    @pl.when(edge)
+    def _():
+        w_across.wait_send()
+        w_inner.wait_send()
+        for j in range(6):
+            e_across(j).wait_send()
+            e_inner(j).wait_send()
+
+    for copy in sent:
+        copy.wait_send()
 
 
 def body(residual, queries, key_value, out_proj, norm_gain, expert_ids, gate_weights, expert_in, expert_down):
@@ -436,25 +537,28 @@
         pltpu.VMEM((4, ROWS, 1024), BF),
         pltpu.VMEM((2, NX, 2, 256, 1024), BF),
         pltpu.VMEM((4, NY, ROWS, 1024), BF),
-        pltpu.VMEM((3, 4, ROWS, 1024), BF),
+        pltpu.VMEM((2, 4, ROWS, 512), BF),
+        pltpu.VMEM((2, 4, ROWS, 1024), BF),
         pltpu.VMEM((ROWS, D), BF),
-        pltpu.VMEM((NX, 2 * CAP, HALF), BF),
-        pltpu.VMEM((3, 2 * CAP, HALF), BF),
-        pltpu.VMEM((NY, EROWS, D), BF),
-        pltpu.VMEM((NY, EROWS, D), BF),
-        pltpu.VMEM((3, EROWS, D), BF),
-        pltpu.VMEM((NX, 2 * CAP, HALF), F32),
-        pltpu.VMEM((3, 2 * CAP, HALF), BF),
-        pltpu.VMEM((2, 2, 192, D), BF),
-        pltpu.VMEM((2, 2, 96, D), BF),
+        pltpu.VMEM((NX, 2 * CAP, 1024), F32),
+        pltpu.VMEM((NX, 2, 2 * CAP, 1024), BF),
+        pltpu.VMEM((3, 2, 2 * CAP, 1024), BF),
+        pltpu.VMEM((2, NY, EROWS, HALF), BF),
+        pltpu.VMEM((2, NY, EROWS, HALF), BF),
+        pltpu.VMEM((2, EROWS, HALF), BF),
+        pltpu.VMEM((2, 2, EROWS, HALF), BF),
+        pltpu.VMEM((NX, 2, 2 * CAP, 1024), BF),
+        pltpu.VMEM((3, 2, 2 * CAP, 1024), BF),
+        pltpu.VMEM((2, 2, 4, 48, D), BF),
+        pltpu.VMEM((2, 2, 2, 48, D), BF),
         sem((5,)),
         sem((7,)), sem, sem((3, 2)),
         sem, sem,
-        sem((14,)), sem, sem((3, 2)), sem((7,)),
-        sem((4, 3)), sem((4, 3)),
-        sem((4,)), sem((4,)),
-        sem((3,)), sem((3,)), sem((3,)), sem((3,)),
-        sem((3,)), sem((3,)), sem((3,)), sem((3,)),
+        sem((15,)), sem, sem((3, 2)), sem((7,)),
+        sem((2, 4)), sem((2, 4)), sem((2, 4)), sem((2, 4)),
+        sem((2, 6)), sem((6,)), sem((2,)), sem((2,)),
+        sem((2, 3)), sem((2, 3)), sem((2, 2)), sem((2, 2)), sem((2,)), sem((2,)),
+        sem((2,)), sem((2,)), sem((2, 2)), sem((2, 2)), sem((2, 3)), sem((2, 3)),
     ]
     return pl.pallas_call(
         kernel,
@@ -474,8 +578,8 @@
         norm_gain.reshape(1, D),
         expert_ids.T,
         gate_weights.T,
-        jnp.swapaxes(expert_in[0], 1, 2),
-        expert_down[0].reshape(2, 96, D),
+        jnp.swapaxes(expert_in[0], 1, 2).reshape(2, 4, 48, D),
+        expert_down[0].reshape(2, 2, 48, D),
     )
 
 

time: 288 us -> 207 us (0.72)
  the two profiles are of different devices: /device:TPU:164 before, /device:TPU:34 now
where the time goes in v2:
time: 207 us
  Pallas kernels  204 us (99%)
  local copies, waits for them, and re-layouts  2.29 us (1%)
    pallas_call x1, Pallas kernels, body(): pl.pallas_call(kernel, out_shape=jax.ShapeDtypeStruct((ROWS, D), BF), in_...  204 us

profile of v2, /device:TPU:34, one launch (start us, length us, event | category | flops | bytes accessed | tf_op | source)
XLA Modules:
  0.0 206.7 jit_solution(4564704101565969404)
XLA Ops:
  0.0 204.4 %layer.1 = bf16[128,4096]{1,0:T(8,128)(2,1)} custom-call(bf16[4,2,128,512]{3,2,1,0:T(8,128)(2,1)} %bitcast.14, bf16[2,64,1024]{2,1,0:T(8,128)(2,1)} %bitcast.16, bf16[2,256,1024]{2,1,0:T(8,128)(2,1)} %bitcast.15, bf16[128,4096]{1,0:T(8,128)(2,1)} %res_ref.1, f32[1,4096]{1,0:T(1,128)} %bitcast.17, s32[8,128]{1,0:T(8,128)} %bitcast.18, f32[8,128]{1,0:T(8,128)} %bitcast.19, ...), custom_call_target="tpu_custom_call" | custom-call | tf_op jit(solution)/shard_map/layer/pallas_call | solution.py:563
  204.4 2.3 %copy.11 = bf16[128,4096]{1,0:T(8,128)(2,1)} copy(bf16[128,4096]{1,0:T(8,128)(2,1)} %layer.1) | data formatting | bytes 2097152

commit v3 on v2

--- a/solution.py
+++ b/solution.py
@@ -25,7 +25,7 @@
     out_ref,
     kvbuf, vext, q2, qown, qother, acc, mrow, att, wbuf, sbuf, oph, rsbuf, stream,
     xsend, packed, xd, disp, down, rop, rnb, back, eb, einbuf, edbuf,
-    loc, s_kv, r_kvz, r_kvx, s_q, r_q, s_w, r_wz, r_wx, r_ws,
+    loc, s_kv, r_kvz, r_kvx, s_q, r_q, s_w, r_wz, r_wx, s_wo, r_wo, r_ws,
     s_op, r_op, s_rs, r_rs, s_e, r_e, s_sib, r_sib, s_x, r_x, s_y, r_y, s_yp, r_yp,
     s_ro, r_ro, s_rn, r_rn, s_rx, r_rx,
 ):
@@ -42,8 +42,8 @@
     edge = (zl == 0) | (zl == 3)
     pair = {"ctx": c, "tp": 2 * y + hp, "dp": d}
     sib = {"ctx": c, "tp": t, "dp": d + 1 - 2 * k}
-    across = {"ctx": c, "tp": 2 * y + hp, "dp": (3 - zl) * 2 + k}
-    inner = {"ctx": c, "tp": t, "dp": (zl + 1 - 2 * (zl % 2)) * 2 + k}
+    near = {"ctx": c, "tp": t, "dp": (zl + 1 - 2 * (zl % 2)) * 2 + k}
+    far = {"ctx": c, "tp": 2 * y + jnp.where(edge, hp, h), "dp": (3 - zl) * 2 + k}
 
     def xpeer(o):
         return {"ctx": lax.rem(c + o, NX), "tp": t, "dp": d}
@@ -63,7 +63,7 @@
         sent.append(copy)
 
     barrier = pltpu.get_barrier_semaphore()
-    peers = [pair, sib, across, inner] + [xpeer(o) for o in (1, 2, 3)] + [ypeer(o) for o in (1, 3)]
+    peers = [pair, sib, near, far] + [xpeer(o) for o in (1, 2, 3)] + [ypeer(o) for o in (1, 3)]
     for dev in peers:
         pl.semaphore_signal(barrier, inc=1, device_id=dev, device_id_type=MESH)
     pl.semaphore_wait(barrier, len(peers))
@@ -92,41 +92,47 @@
     ed_loc = pltpu.make_async_copy(ed_ref, edbuf.at[h], loc.at[4])
     ed_loc.start()
 
-    w_across = rcopy(w_ref.at[k], wbuf.at[h, c, k], s_w.at[0], r_wz, across)
-    w_inner = rcopy(wbuf.at[hp, c, k], wbuf.at[hp, c, k], s_w.at[14], r_wz, inner)
-
-    @pl.when(edge)
-    def _():
-        w_across.start()
+    w_pair = rcopy(w_ref.at[k], wbuf.at[h, c, k], s_w.at[0], r_wz, pair)
 
     vext[:, :, HD:] = jnp.ones((NX, 1024, HD), BF)
 
-    def spread_q(src, which):
+    def spread_q(src, which, heads):
         for b in range(4):
             block = src[b]
-            for j in range(4):
-                q2[which, j, b] = block[:, j * HD : (j + 1) * HD]
+            for n, j in enumerate(heads):
+                q2[which, j, b] = block[:, n * HD : (n + 1) * HD]
 
     q_loc.wait()
-    spread_q(qown, h)
-
-    q_pair = rcopy(q_ref.at[:, hp], qother, s_q, r_q, pair)
+    spread_q(qown, h, range(4))
+
+    def q_pair(n):
+        return rcopy(
+            q_ref.at[:, hp, :, pl.ds(256 * n, 256)], qother.at[n], s_q.at[n], r_q.at[n], pair
+        )
+
     kv_loc.wait()
     kv_pair.wait_recv()
-    q_pair.start()
     for o in (1, 2, 3):
         pl.when(c + o < NX)(lambda o=o: kv_fwd(o).start())
+    go(q_pair(0))
+    go(w_pair)
+    go(q_pair(1))
 
     def put_v(src):
         vext[src, :, :HD] = kvbuf[src, 1].reshape(HD, 1024).astype(F32).T.astype(BF)
 
     put_v(c)
     def w_own(o):
-        return rcopy(w_ref.at[k], wbuf.at[h, c, k], s_w.at[o], r_wx.at[o - 1, 0], xpeer(o))
+        return rcopy(w_ref.at[k], wbuf.at[h, c, k], s_w.at[o], r_wx.at[o // 2, 0], xpeer(o))
 
     def w_fwd(o):
-        return rcopy(
-            wbuf.at[hp, c, k], wbuf.at[hp, c, k], s_w.at[3 + o], r_wx.at[o - 1, 1], xpeer(o)
+        part = wbuf.at[hp, c, k]
+        return rcopy(part, part, s_w.at[3 + o], r_wx.at[o // 2, 1], xpeer(o))
+
+    def w_opp(side, which):
+        part = wbuf.at[hp if which else h, lax.rem(c + 3 - 2 * side, NX), k, side]
+        return rcopy(
+            part, part, s_wo.at[side, which], r_wo.at[side, which], xpeer(1 + 2 * side)
         )
 
     w_sib = rcopy(wbuf.at[hp, c, k], wbuf.at[hp, c, k], s_w.at[7], r_ws.at[0], sib)
@@ -147,12 +153,12 @@
     def e_across(j):
         return rcopy(
             e_part(ein_ref, ed_ref, j, None), e_part(einbuf, edbuf, j, h),
-            s_e.at[0, j], r_e.at[j], across,
+            s_e.at[0, j], r_e.at[j], far,
         )
 
     def e_inner(j):
         part = e_part(einbuf, edbuf, j, hp)
-        return rcopy(part, part, s_e.at[1, j], r_e.at[j], inner)
+        return rcopy(part, part, s_e.at[1, j], r_e.at[j], near)
 
     def e_pass(j):
         @pl.when(edge)
@@ -163,28 +169,29 @@
     ein_sib = rcopy(einbuf.at[k, hp], einbuf.at[k, hp], s_sib.at[0], r_sib.at[0], sib)
     ed_sib = rcopy(edbuf.at[hp, k], edbuf.at[hp, k], s_sib.at[1], r_sib.at[1], sib)
 
-    row_at = lax.broadcasted_iota(jnp.int32, (4, ROWS, 256), 1).reshape(4 * ROWS, 256) + h * ROWS
-    col_at = lax.broadcasted_iota(jnp.int32, (4 * ROWS, 256), 1)
+    row_at = lax.broadcasted_iota(jnp.int32, (2, ROWS, 256), 1).reshape(2 * ROWS, 256) + h * ROWS
+    col_at = lax.broadcasted_iota(jnp.int32, (2 * ROWS, 256), 1)
     allowed = col_at <= row_at
 
-    def diagonal(which):
+    def diagonal(which, j0):
         keys = kvbuf[c, 0].reshape(HD, 1024)
         for b in range(4):
             kl = (b + 1) * 256
-            qs = q2[which, :, b].reshape(4 * ROWS, HD)
+            qs = q2[which, pl.ds(j0, 2), b].reshape(2 * ROWS, HD)
             s = jnp.dot(qs, keys[:, :kl], preferred_element_type=F32)
             last = jnp.where(allowed, s[:, kl - 256 :], -1e30)
             s = last if b == 0 else jnp.concatenate([s[:, : kl - 256], last], axis=1)
-            top = jnp.broadcast_to(jnp.max(s, axis=1, keepdims=True) * SCALE2, (4 * ROWS, HD))
+            top = jnp.broadcast_to(jnp.max(s, axis=1, keepdims=True) * SCALE2, (2 * ROWS, HD))
             p = jnp.exp2(s * SCALE2 - jnp.concatenate([top] * (kl // HD), axis=1)).astype(BF)
-            acc[which, :, b] = jnp.dot(
+            acc[which, pl.ds(j0, 2), b] = jnp.dot(
                 p, vext[c, :kl], preferred_element_type=F32
-            ).reshape(4, ROWS, 2 * HD)
-            mrow[which, :, b] = top.reshape(4, ROWS, HD)
-
-    def full_block(which, src):
+            ).reshape(2, ROWS, 2 * HD)
+            mrow[which, pl.ds(j0, 2), b] = top.reshape(2, ROWS, HD)
+
+    def full_block(which, j0, src):
         keys = kvbuf[src, 0].reshape(HD, 1024)
-        for j in range(4):
+        for n in range(2):
+            j = j0 + n
             qs = q2[which, j].reshape(4 * ROWS, HD)
             s = jnp.dot(qs, keys, preferred_element_type=F32)
             old = mrow[which, j].reshape(4 * ROWS, HD)
@@ -199,37 +206,29 @@
             mrow[which, j] = top.reshape(4, ROWS, HD)
 
     def group(g, carry):
-        which = lax.rem(h + g, 2)
-
-        @pl.when(g == 1)
+        which = lax.rem(h + g // 2, 2)
+        j0 = 2 * (g % 2)
+
+        @pl.when(g == 2)
         def _():
-            q_pair.wait_recv()
-            @pl.when(jnp.logical_not(edge))
-            def _():
-                w_across.wait_recv()
-
-            for o in (1, 3, 2):
+            q_pair(0).wait_recv()
+            spread_q(qother.at[0], hp, (0, 1))
+
+        @pl.when(g == 3)
+        def _():
+            w_pair.wait_recv()
+            for o in (1, 3):
                 w_fwd(o).start()
             w_sib.start()
+            q_pair(1).wait_recv()
+            spread_q(qother.at[1], hp, (2, 3))
 
             @pl.when(edge)
             def _():
                 for j in range(6):
                     e_across(j).start()
 
-            spread_q(qother, hp)
-
-        diagonal(which)
-
-        @pl.when(g == 0)
-        def _():
-            for o in (1, 3, 2):
-                w_own(o).start()
-
-            @pl.when(edge)
-            def _():
-                w_across.wait_recv()
-                w_inner.start()
+        diagonal(which, j0)
 
         def earlier(o, carry):
             src = c - o
@@ -244,13 +243,26 @@
                 ).wait_recv()
                 put_v(src)
 
-            full_block(which, src)
+            full_block(which, j0, src)
             return carry
 
         lax.fori_loop(1, c + 1, earlier, 0)
+
+        @pl.when(g == 0)
+        def _():
+            for o in (1, 2, 3):
+
+                @pl.when(c + o < NX)
+                def _(o=o):
+                    kv_own(o).wait_send()
+                    kv_fwd(o).wait_send()
+
+            for o in (1, 3):
+                w_own(o).start()
+
         return carry
 
-    lax.fori_loop(0, 2, group, 0)
+    lax.fori_loop(0, 4, group, 0)
 
     for w in range(2):
         for j in range(4):
@@ -258,9 +270,9 @@
             head = (whole[:, :HD] / whole[:, HD:]).astype(BF)
             att[:, :, (4 * w + j) * HD : (4 * w + j + 1) * HD] = head.reshape(4, ROWS, HD)
 
-    e_pass(0)
-    for o in (1, 3, 2):
+    for o in (1, 3):
         w_own(o).wait_recv()
+        go(w_opp(o // 2, 0))
         w_sib_own(o).start()
     w_loc.wait()
     w_sib.wait_recv()
@@ -277,29 +289,7 @@
             s_rs.at[side, i], r_rs.at[side, i], ypeer(1 + 2 * side),
         )
 
-    order = (0, 1, 3, 2)
-    for i, o in enumerate(order):
-        cs = lax.rem(c + NX - o, NX)
-        if o:
-            w_fwd(o).wait_recv()
-            w_sib_fwd(o).start()
-            w_sib_own(o).wait_recv()
-            w_sib_fwd(o).wait_recv()
-
-        def tile(n, carry, cs=cs, i=i):
-            at = pl.ds(pl.multiple_of(n * 256, 256), 256)
-            rows = att[...].reshape(4 * ROWS, 1024)
-            w0 = jnp.concatenate([wbuf[0, cs, 0, :, at], wbuf[0, cs, 1, :, at]], axis=0)
-            w1 = jnp.concatenate([wbuf[1, cs, 0, :, at], wbuf[1, cs, 1, :, at]], axis=0)
-            part = jnp.dot(rows[:, :512], w0, preferred_element_type=F32)
-            part = part + jnp.dot(rows[:, 512:], w1, preferred_element_type=F32)
-            sbuf[i, :, :, at] = part.astype(BF).reshape(4, ROWS, 256)
-            return carry
-
-        lax.fori_loop(0, 4, tile, 0)
-        for side in range(2):
-            go(op_copy(i, side))
-    for i in range(4):
+    def add_own(i):
         for side in range(2):
             op_copy(i, side).wait_recv()
             to = lax.rem(y + 1 + 2 * side, NY)
@@ -308,7 +298,43 @@
                 sbuf[i, to, :, lo : lo + 512].astype(F32) + oph[side, i].astype(F32)
             ).astype(BF)
             go(nb_copy(i, side))
-    e_pass(1)
+
+    order = (0, 1, 3, 2)
+    for i, o in enumerate(order):
+        cs = lax.rem(c + NX - o, NX)
+        if i == 1:
+            for n in (1, 3):
+                w_fwd(n).wait_recv()
+                go(w_opp(n // 2, 1))
+                w_sib_fwd(n).start()
+        if i == 3:
+            add_own(2)
+            for which in range(2):
+                for side in range(2):
+                    w_opp(side, which).wait_recv()
+            w_sib_own(o).start()
+            w_sib_fwd(o).start()
+        if i:
+            w_sib_own(o).wait_recv()
+            w_sib_fwd(o).wait_recv()
+
+        def tile(n, carry, cs=cs, i=i):
+            at = pl.ds(pl.multiple_of(n * 256, 256), 256)
+            rows = att[...].reshape(4 * ROWS, 1024)
+            w0 = wbuf[0, cs, :, :, :, at].reshape(512, 256)
+            w1 = wbuf[1, cs, :, :, :, at].reshape(512, 256)
+            part = jnp.dot(rows[:, :512], w0, preferred_element_type=F32)
+            part = part + jnp.dot(rows[:, 512:], w1, preferred_element_type=F32)
+            sbuf[i, :, :, at] = part.astype(BF).reshape(4, ROWS, 256)
+            return carry
+
+        lax.fori_loop(0, 4, tile, 0)
+        for side in range(2):
+            go(op_copy(i, side))
+        if i in (1, 2):
+            add_own(i - 1)
+    add_own(3)
+    e_pass(0)
 
     slot_at = lax.broadcasted_iota(jnp.int32, (ROWS, ROWS), 0)
     lane_at = lax.broadcasted_iota(jnp.int32, (ROWS, ROWS), 1)
@@ -340,8 +366,8 @@
         stream[:, at] = block
         wide = block.astype(F32)
         square = square + jnp.sum(wide * wide, axis=1, keepdims=True)
-        if i in (1, 2):
-            e_pass(1 + i)
+        if i in (1, 3):
+            e_pass(1 + i // 2)
     inv = lax.rsqrt(square * (1.0 / D) + 1e-6)
 
     def x_copy(half, o):
@@ -378,7 +404,7 @@
         packed[:, half] = xsend[...].astype(BF)
         for o in (2, 1, 3):
             go(x_copy(half, o))
-    e_pass(4)
+    e_pass(3)
     for half in range(2):
         for o in (1, 3, 2):
             x_copy(half, o).wait_recv()
@@ -387,7 +413,7 @@
             disp[half, 0, :, n * 1024 : (n + 1) * 1024] = merge(pieces, n, [])
         for side in range(2):
             go(y_copy(half, side))
-    e_pass(5)
+        e_pass(4 + half)
 
     @pl.when(jnp.logical_not(edge))
     def _():
@@ -404,25 +430,29 @@
     ed_loc.wait()
     ein_sib.wait_recv()
     ed_sib.wait_recv()
-    y_copy(0, 1).wait_recv()
-    y_copy(1, 0).wait_recv()
-    y_pass(0).wait_recv()
-    y_pass(1).wait_recv()
-
-    def project_in(n):
+
+    def project_in(n, half):
         total = jnp.zeros((4 * EROWS, 384), F32)
-        for kk in range(4):
-            lo = (kk % 2) * 1024
+        for kk in range(2):
+            lo = kk * 1024
+            at = half * HALF + lo
             total = total + lax.dot_general(
-                disp[kk // 2, :, :, lo : lo + 1024].reshape(4 * EROWS, 1024),
-                einbuf[n, :, :, :, kk * 1024 : (kk + 1) * 1024].reshape(384, 1024),
+                disp[half, :, :, lo : lo + 1024].reshape(4 * EROWS, 1024),
+                einbuf[n, :, :, :, at : at + 1024].reshape(384, 1024),
                 NT,
                 preferred_element_type=F32,
             )
         return total
 
-    gate_part = project_in(0)
-    hidden = (gate_part / (1.0 + jnp.exp(-gate_part)) * project_in(1)).astype(BF)
+    y_copy(0, 1).wait_recv()
+    y_pass(0).wait_recv()
+    gate_part = project_in(0, 0)
+    up_part = project_in(1, 0)
+    y_copy(1, 0).wait_recv()
+    y_pass(1).wait_recv()
+    gate_part = gate_part + project_in(0, 1)
+    up_part = up_part + project_in(1, 1)
+    hidden = (gate_part / (1.0 + jnp.exp(-gate_part)) * up_part).astype(BF)
 
     def ro_copy(half):
         return rcopy(
@@ -495,25 +525,16 @@
             out_ref[:, at] = (stream[:, at].astype(F32) + added).astype(BF)
 
     kv_pair.wait_send()
-    for o in (1, 2, 3):
-
-        @pl.when(c + o < NX)
-        def _(o=o):
-            kv_own(o).wait_send()
-            kv_fwd(o).wait_send()
-
-    q_pair.wait_send()
     w_sib.wait_send()
     for o in (1, 2, 3):
-        w_own(o).wait_send()
-        w_fwd(o).wait_send()
+        if o != 2:
+            w_own(o).wait_send()
+            w_fwd(o).wait_send()
         w_sib_own(o).wait_send()
         w_sib_fwd(o).wait_send()
 
     @pl.when(edge)
     def _():
-        w_across.wait_send()
-        w_inner.wait_send()
         for j in range(6):
             e_across(j).wait_send()
             e_inner(j).wait_send()
@@ -531,11 +552,11 @@
         pltpu.VMEM((NX, 1024, 2 * HD), BF),
         pltpu.VMEM((2, 4, 4, ROWS, HD), BF),
         pltpu.VMEM((4, ROWS, 512), BF),
-        pltpu.VMEM((4, ROWS, 512), BF),
+        pltpu.VMEM((2, 4, ROWS, 256), BF),
         pltpu.VMEM((2, 4, 4, ROWS, 2 * HD), F32),
         pltpu.VMEM((2, 4, 4, ROWS, HD), F32),
         pltpu.VMEM((4, ROWS, 1024), BF),
-        pltpu.VMEM((2, NX, 2, 256, 1024), BF),
+        pltpu.VMEM((2, NX, 2, 2, ROWS, 1024), BF),
         pltpu.VMEM((4, NY, ROWS, 1024), BF),
         pltpu.VMEM((2, 4, ROWS, 512), BF),
         pltpu.VMEM((2, 4, ROWS, 1024), BF),
@@ -553,8 +574,8 @@
         pltpu.VMEM((2, 2, 2, 48, D), BF),
         sem((5,)),
         sem((7,)), sem, sem((3, 2)),
-        sem, sem,
-        sem((15,)), sem, sem((3, 2)), sem((7,)),
+        sem((2,)), sem((2,)),
+        sem((14,)), sem, sem((2, 2)), sem((2, 2)), sem((2, 2)), sem((7,)),
         sem((2, 4)), sem((2, 4)), sem((2, 4)), sem((2, 4)),
         sem((2, 6)), sem((6,)), sem((2,)), sem((2,)),
         sem((2, 3)), sem((2, 3)), sem((2, 2)), sem((2, 2)), sem((2,)), sem((2,)),
@@ -573,7 +594,7 @@
     )(
         queries.reshape(4, 2, ROWS, 512),
         jnp.swapaxes(key_value, 1, 2),
-        out_proj.reshape(2, 256, 1024),
+        out_proj.reshape(2, 2, ROWS, 1024),
         residual,
         norm_gain.reshape(1, D),
         expert_ids.T,

time: 207 us -> 201 us (0.971)
  Pallas kernels: 204 us -> 199 us
    pallas_call x1, Pallas kernels: 204 us -> 199 us  [body(): pl.pallas_call(kernel, out_shape=jax.ShapeDtypeStruct((ROWS, D), BF), in_...]
where the time goes in v3:
time: 201 us
  Pallas kernels  199 us (99%)
  local copies, waits for them, and re-layouts  2.29 us (1%)
    pallas_call x1, Pallas kernels, body(): pl.pallas_call(kernel, out_shape=jax.ShapeDtypeStruct((ROWS, D), BF), in_...  199 us

profile of v3, /device:TPU:34, one launch (start us, length us, event | category | flops | bytes accessed | tf_op | source)
XLA Modules:
  0.0 200.9 jit_solution(4406779310663923895)
XLA Ops:
  0.0 198.6 %layer.1 = bf16[128,4096]{1,0:T(8,128)(2,1)} custom-call(bf16[4,2,128,512]{3,2,1,0:T(8,128)(2,1)} %bitcast.14, bf16[2,64,1024]{2,1,0:T(8,128)(2,1)} %bitcast.16, bf16[2,2,128,1024]{3,2,1,0:T(8,128)(2,1)} %bitcast.15, bf16[128,4096]{1,0:T(8,128)(2,1)} %res_ref.1, f32[1,4096]{1,0:T(1,128)} %bitcast.17, s32[8,128]{1,0:T(8,128)} %bitcast.18, f32[8,128]{1,0:T(8,128)} %bitcast.19, ...), custom_call_target="tpu_custom_call" | custom-call | tf_op jit(solution)/shard_map/layer/pallas_call | solution.py:584
  198.6 2.3 %copy.11 = bf16[128,4096]{1,0:T(8,128)(2,1)} copy(bf16[128,4096]{1,0:T(8,128)(2,1)} %layer.1) | data formatting | bytes 2097152

commit v4 on v3

--- a/solution.py
+++ b/solution.py
@@ -377,13 +377,13 @@
 
     def y_copy(half, side):
         return rcopy(
-            disp.at[half, 0], disp.at[half, 1 + 2 * side], s_y.at[half, side], r_y.at[half, side],
+            disp.at[half, 0], disp.at[half, 1 + side], s_y.at[half, side], r_y.at[half, side],
             ypeer(1 + 2 * side),
         )
 
     def y_pass(half):
         return rcopy(
-            disp.at[half, 1 + 2 * half], disp.at[half, 2], s_yp.at[half], r_yp.at[half],
+            disp.at[half, 1 + half], disp.at[half, 3], s_yp.at[half], r_yp.at[half],
             ypeer(1 + 2 * half),
         )
 
@@ -431,13 +431,14 @@
     ein_sib.wait_recv()
     ed_sib.wait_recv()
 
-    def project_in(n, half):
-        total = jnp.zeros((4 * EROWS, 384), F32)
+    def project_in(n, half, lo_slot, hi_slot):
+        rows = (hi_slot - lo_slot) * EROWS
+        total = jnp.zeros((rows, 384), F32)
         for kk in range(2):
             lo = kk * 1024
             at = half * HALF + lo
             total = total + lax.dot_general(
-                disp[half, :, :, lo : lo + 1024].reshape(4 * EROWS, 1024),
+                disp[half, lo_slot:hi_slot, :, lo : lo + 1024].reshape(rows, 1024),
                 einbuf[n, :, :, :, at : at + 1024].reshape(384, 1024),
                 NT,
                 preferred_element_type=F32,
@@ -446,22 +447,24 @@
 
     y_copy(0, 1).wait_recv()
     y_pass(0).wait_recv()
-    gate_part = project_in(0, 0)
-    up_part = project_in(1, 0)
+    parts = [project_in(n, 0, 0, 4) for n in range(2)]
     y_copy(1, 0).wait_recv()
+    parts_near = [project_in(n, 1, 0, 3) for n in range(2)]
     y_pass(1).wait_recv()
-    gate_part = gate_part + project_in(0, 1)
-    up_part = up_part + project_in(1, 1)
+    gate_part, up_part = [
+        parts[n] + jnp.concatenate([parts_near[n], project_in(n, 1, 3, 4)], axis=0)
+        for n in range(2)
+    ]
     hidden = (gate_part / (1.0 + jnp.exp(-gate_part)) * up_part).astype(BF)
 
     def ro_copy(half):
         return rcopy(
-            down.at[half, 2], rop.at[half], s_ro.at[half], r_ro.at[half], ypeer(1 + 2 * half)
+            down.at[half, 3], rop.at[half], s_ro.at[half], r_ro.at[half], ypeer(1 + 2 * half)
         )
 
     def rn_copy(half, side):
         return rcopy(
-            down.at[half, 3 - 2 * side], rnb.at[half, side], s_rn.at[half, side],
+            down.at[half, 2 - side], rnb.at[half, side], s_rn.at[half, side],
             r_rn.at[half, side], ypeer(1 + 2 * side),
         )
 
@@ -482,7 +485,7 @@
             go(ro_copy(1))
     for half in range(2):
         ro_copy(half).wait_recv()
-        slot = 3 - 2 * half
+        slot = 2 - half
         down[half, slot] = (down[half, slot].astype(F32) + rop[half].astype(F32)).astype(BF)
         go(rn_copy(half, half))
         if half == 0:

time: 201 us -> 202 us (level)
  no operation moved by 1% of the time
where the time goes in v4:
time: 202 us
  Pallas kernels  199 us (99%)
  local copies, waits for them, and re-layouts  2.29 us (1%)
    pallas_call x1, Pallas kernels, body(): pl.pallas_call(kernel, out_shape=jax.ShapeDtypeStruct((ROWS, D), BF), in_...  199 us

profile of v4, /device:TPU:34, one launch (start us, length us, event | category | flops | bytes accessed | tf_op | source)
XLA Modules:
  0.0 201.6 jit_solution(6153868064657158349)
XLA Ops:
  0.0 199.3 %layer.1 = bf16[128,4096]{1,0:T(8,128)(2,1)} custom-call(bf16[4,2,128,512]{3,2,1,0:T(8,128)(2,1)} %bitcast.14, bf16[2,64,1024]{2,1,0:T(8,128)(2,1)} %bitcast.16, bf16[2,2,128,1024]{3,2,1,0:T(8,128)(2,1)} %bitcast.15, bf16[128,4096]{1,0:T(8,128)(2,1)} %res_ref.1, f32[1,4096]{1,0:T(1,128)} %bitcast.17, s32[8,128]{1,0:T(8,128)} %bitcast.18, f32[8,128]{1,0:T(8,128)} %bitcast.19, ...), custom_call_target="tpu_custom_call" | custom-call | tf_op jit(solution)/shard_map/layer/pallas_call | solution.py:587
  199.4 2.3 %copy.11 = bf16[128,4096]{1,0:T(8,128)(2,1)} copy(bf16[128,4096]{1,0:T(8,128)(2,1)} %layer.1) | data formatting | bytes 2097152
